TPU v7x, 32 devices: a whole 2x2x4 slice. The times are simulated.
32 devices in a mesh: dp: 8 (over y, x, core), expert: 4 (over z).
Axes of the slice: x: 2, y: 2, z: 4, core: 2. Of those that a mesh axis runs over, the one named last changes fastest.
Arguments:
- tokens: bfloat16 [512, 2048], P(('dp', 'expert')), may hold values from -6 to 6
- out_grad: bfloat16 [512, 2048], P(('dp', 'expert')), may hold values from -6 to 6
- gate_weights: bfloat16 [512, 2], P(('dp', 'expert')), may hold values from 0.049804688 to 1
- expert_ids: int32 [512, 2], P(('dp', 'expert')), may hold values from 0 to 3, all different within a row; in each aligned block of 16 rows (0 to 15, 16 to 31, ...) at most 10 rows name the same one
- swapped: int32 [4], replicated, may hold values from 0 to 1, as said below
- up_weight: bfloat16 [4, 2048, 384], P('expert'), may hold values from -0.125 to 0.125
- down_weight: bfloat16 [4, 384, 2048], P('expert'), may hold values from -0.3125 to 0.3125
Outputs:
- layer_out: bfloat16 [512, 2048], P(('dp', 'expert'))
- token_grad: bfloat16 [512, 2048], P(('dp', 'expert'))
- up_grad: float32 [4, 2048, 384], P('expert', 'dp')
- down_grad: float32 [4, 384, 2048], P('expert', 'dp')
Inputs may be any that keep to these rules, and one draw needn't show every extreme that they name: swapped[s] equals swapped[(s + 2) mod 4]; swapped[0] is 1. `expert_ids`: A token's 2 experts differ; at most 10 of the tokens of one device name one expert, and that many in some device.
All inputs are finite; a program needn't handle non-finite values.
Results may differ from a plain program's by a relative error of at most 0.023.
Values may be sent and summed in bfloat16 or wider, within the bound.
A program may use at most 64 MiB of HBM per device.

v0:
```python
import jax
import jax.numpy as jnp
from jax import lax
from jax.sharding import PartitionSpec as P

BF = jnp.bfloat16
F32 = jnp.float32


def on_device(tokens, out_grad, gate_weights, expert_ids, swapped, up_weight, down_weight):
    owners = lax.axis_size("expert")
    mine = lax.axis_index("expert")
    width = tokens.shape[1]
    lanes = jnp.arange(128, dtype=jnp.int32)
    hit = expert_ids[:, :, None] == lanes[None, None, :]
    gates = jnp.sum(jnp.where(hit, gate_weights.astype(F32)[:, :, None], 0.0), axis=1).astype(BF)
    packed = jnp.concatenate([tokens, out_grad, gates], axis=1)
    full = lax.all_gather(packed, "expert", axis=0, tiled=True)
    x, og, gates = (full[:, :width], full[:, width : 2 * width], full[:, 2 * width :])
    gates = gates.astype(F32)
    flag = lax.dynamic_slice_in_dim(swapped, mine, 1, 0)[0] == 1
    held = jnp.where(flag, (mine + owners // 2) % owners, mine)

    def column(e):
        return jnp.sum(jnp.where(lanes[None, :] == e, gates, 0.0), axis=1, keepdims=True)

    gate = column(mine)
    up, down = (up_weight[0], down_weight[0])
    dy = (gate * og.astype(F32)).astype(BF)
    hidden = jnp.dot(x, up, preferred_element_type=F32)
    d_active = lax.dot_general(dy, down, (((1,), (1,)), ((), ())), preferred_element_type=F32)
    sigma = jax.nn.sigmoid(hidden)
    active = jnp.where(gate > 0, hidden * sigma, 0.0).astype(BF)
    d_hidden = (d_active * sigma * (1.0 + hidden * (1.0 - sigma))).astype(BF)
    other = lax.ppermute(
        jnp.concatenate([active, d_hidden], axis=1),
        "expert",
        [(i, (i + owners // 2) % owners) for i in range(owners)],
    )
    y = jnp.dot(active, down, preferred_element_type=F32).astype(BF).astype(F32)
    dx = lax.dot_general(d_hidden, up, (((1,), (1,)), ((), ())), preferred_element_type=F32)
    back = jnp.concatenate([(gate * y).astype(BF), dx.astype(BF)], axis=1)
    back = lax.psum_scatter(back, "expert", scatter_dimension=0, tiled=True)
    fw = active.shape[1]
    act_h = jnp.where(flag, other[:, :fw], active)
    dh_h = jnp.where(flag, other[:, fw:], d_hidden)
    dy_h = (column(held) * og.astype(F32)).astype(BF)
    over = (((0,), (0,)), ((), ()))
    part_up = lax.dot_general(x, dh_h, over, preferred_element_type=F32).astype(BF)
    part_down = lax.dot_general(act_h, dy_h, over, preferred_element_type=F32).astype(BF)
    sum_up = lax.psum_scatter(part_up, "dp", scatter_dimension=0, tiled=True).astype(F32)
    sum_down = lax.psum_scatter(part_down, "dp", scatter_dimension=0, tiled=True).astype(F32)
    return (back[:, :width], back[:, width:], sum_up[None], sum_down[None])


def solution(mesh):
    rows = P(("dp", "expert"), None)
    in_specs = (rows, rows, rows, rows, P(), P("expert", None, None), P("expert", None, None))
    out_specs = (rows, rows, P("expert", "dp", None), P("expert", "dp", None))
    return jax.shard_map(
        on_device, mesh=mesh, in_specs=in_specs, out_specs=out_specs, check_vma=False
    )
```

profile of v0, /device:TPU:0, one launch (start us, length us, event | category | flops | bytes accessed | tf_op | source)
XLA Modules:
  0.0 145.8 jit_solution(18337395478298540508)
XLA Ops:
  7.2 0.0 reduce-scatter.4.cloned.1.call-start
  7.2 1.3 dynamic_slice.3
  9.3 0.8 convert_element_type.45
  10.0 0.8 select_reduce_fusion
  10.8 0.9 pad_maximum_fusion.1
  11.7 17.5 %all_gather.3 = bf16[64,4224]{1,0:T(8,128)(2,1)S(1)} all-gather(bf16[16,4224]{1,0:T(8,128)(2,1)S(1)} %pad_maximum_fusion.1), channel_id=1, replica_groups=mesh['dp'=8,'expert'=4] {'expert'}, dimensions={0}, use_global_device_ids=true | all-gather | bytes 675840 | tf_op jit(solution)/shard_map/all_gather | solution.py:18
  29.2 0.1 fusion.31
  29.3 0.4 select_convert_fusion
  29.7 0.6 fusion.15
  30.3 0.4 fusion.2
  30.8 0.6 convolution_convert_fusion.2
  31.4 0.8 pad_maximum_fusion
  32.2 0.0 reduce-scatter.8.cloned.1.call-start
  32.3 0.8 collective-permute-start
  33.1 4.8 %collective-permute-done = bf16[64,768]{1,0:T(8,128)(2,1)S(1)} collective-permute-done((bf16[64,768]{1,0:T(8,128)(2,1)S(1)}, bf16[64,768]{1,0:T(8,128)(2,1)S(1)}, u32[]{:S(2)}, u32[]{:S(2)}) %collective-permute-start) | collective-permute-done | bytes 98336 | tf_op jit(solution)/shard_map/ppermute | solution.py:35
  37.9 1.8 %convolution_convert_fusion = bf16[384,2048]{1,0:T(8,128)(2,1)} fusion(f32[64]{0:T(128)S(1)} %get-tuple-element.4, bf16[64,4224]{1,0:T(8,128)(2,1)S(1)} %all_gather.3, bf16[64,384]{1,0:T(8,128)(2,1)S(1)} %get-tuple-element.8, bf16[64,768]{1,0:T(8,128)(2,1)S(1)} %collective-permute-done, pred[]{:T(512)} %bitcast.2), kind=kOutput, calls=%fused_computation | convolution fusion | flops 101867520 | bytes 1933825 | tf_op jit(solution)/shard_map/dot_general | solution.py:50
  39.7 0.0 reduce-scatter.6.cloned.1.call-start
  39.7 1.8 %convolution_convert_fusion.1 = bf16[2048,384]{1,0:T(8,128)(2,1)} fusion(bf16[64,4224]{1,0:T(8,128)(2,1)S(1)} %all_gather.3, bf16[64,384]{1,0:T(8,128)(2,1)S(1)} %fusion.15, bf16[64,768]{1,0:T(8,128)(2,1)S(1)} %collective-permute-done, pred[]{:T(512)} %bitcast.2), kind=kOutput, calls=%fused_computation.1 | convolution fusion | flops 101474304 | bytes 1933313 | tf_op jit(solution)/shard_map/dot_general | solution.py:49
  41.5 14.2 %reduce-scatter.4.cloned.1.call-done = bf16[16,4096]{1,0:T(8,128)(2,1)} async-done(((bf16[64,4096]{1,0:T(8,128)(2,1)}), bf16[16,4096]{1,0:T(8,128)(2,1)}) %reduce-scatter.4.cloned.1.call-update) | async-done | bytes 131088 | tf_op jit(solution)/shard_map/reduce_scatter | solution.py:43
  55.8 1.5 %fusion.32 = (bf16[16,2048]{1,0:T(8,128)(2,1)}, bf16[16,2048]{1,0:T(8,128)(2,1)}) fusion(bf16[16,4096]{1,0:T(8,128)(2,1)} %reduce-scatter.4.cloned.1.call-done), kind=kLoop, calls=%fused_computation.46 | loop fusion | bytes 262144 | tf_op jit(solution)/shard_map/slice | solution.py:53
  57.3 38.5 %reduce-scatter.8.cloned.1.call-done = bf16[48,2048]{1,0:T(8,128)(2,1)} async-done(((bf16[384,2048]{1,0:T(8,128)(2,1)}), bf16[48,2048]{1,0:T(8,128)(2,1)}) %reduce-scatter.8.cloned.1.call-update) | async-done | bytes 196624 | tf_op jit(solution)/shard_map/reduce_scatter | solution.py:52
  95.8 1.7 %bitcast_convert_fusion = f32[1,48,2048]{2,1,0:T(8,128)} fusion(bf16[48,2048]{1,0:T(8,128)(2,1)} %reduce-scatter.8.cloned.1.call-done), kind=kLoop, calls=%fused_computation.27 | loop fusion | flops 98304 | bytes 589824 | tf_op jit(solution)/shard_map/broadcast_in_dim | solution.py:53
  97.5 40.1 %reduce-scatter.6.cloned.1.call-done = bf16[256,384]{1,0:T(8,128)(2,1)} async-done(((bf16[2048,384]{1,0:T(8,128)(2,1)}), bf16[256,384]{1,0:T(8,128)(2,1)}) %reduce-scatter.6.cloned.1.call-update) | async-done | bytes 196624 | tf_op jit(solution)/shard_map/reduce_scatter | solution.py:51
  137.6 1.7 %bitcast_convert_fusion.1 = f32[1,256,384]{2,1,0:T(8,128)} fusion(bf16[256,384]{1,0:T(8,128)(2,1)} %reduce-scatter.6.cloned.1.call-done), kind=kLoop, calls=%fused_computation.28 | loop fusion | flops 98304 | bytes 589824 | tf_op jit(solution)/shard_map/broadcast_in_dim | solution.py:53
  (10 shorter events, 0.1 us)
Async XLA Ops:
  7.2 22.2 %copy-start = (bf16[1,2048,384]{2,1,0:T(8,128)(2,1)S(1)}, bf16[1,2048,384]{2,1,0:T(8,128)(2,1)}, u32[]{:S(2)}) copy-start(bf16[1,2048,384]{2,1,0:T(8,128)(2,1)} %param.12) | copy-start | bytes 4718596
  7.2 48.6 %reduce-scatter.4.cloned.1.call-start = ((), (), s32[]{:S(2)}) async-start(), calls=%async_computation.3 | async-start | bytes 655360 | tf_op jit(solution)/shard_map/reduce_scatter | solution.py:43
  9.2 20.5 %copy-start.1 = (bf16[1,384,2048]{2,1,0:T(8,128)(2,1)S(1)}, bf16[1,384,2048]{2,1,0:T(8,128)(2,1)}, u32[]{:S(2)}) copy-start(bf16[1,384,2048]{2,1,0:T(8,128)(2,1)} %param.13) | copy-start | bytes 4718596
  32.2 63.6 %reduce-scatter.8.cloned.1.call-start = ((), (), s32[]{:S(2)}) async-start(), calls=%async_computation.5 | async-start | bytes 1769472 | tf_op jit(solution)/shard_map/reduce_scatter | solution.py:52
  32.3 5.6 %collective-permute-start = (bf16[64,768]{1,0:T(8,128)(2,1)S(1)}, bf16[64,768]{1,0:T(8,128)(2,1)S(1)}, u32[]{:S(2)}, u32[]{:S(2)}) collective-permute-start(bf16[64,768]{1,0:T(8,128)(2,1)S(1)} %pad_maximum_fusion.2), channel_id=1, source_target_pairs={{0,2},{1,3},{2,0},{3,1},{4,6},{5,7},{6,4},{7,5},{8,10},{9,11},{10,... | collective-permute-start | bytes 294920 | tf_op jit(solution)/shard_map/ppermute | solution.py:35
  39.7 97.9 %reduce-scatter.6.cloned.1.call-start = ((), (), s32[]{:S(2)}) async-start(), calls=%async_computation.4 | async-start | bytes 1769472 | tf_op jit(solution)/shard_map/reduce_scatter | solution.py:51
Sparse Core Ops, SparseCore 0:
  32.3 23.3 reduce-scatter.3
  59.1 36.7 reduce-scatter.7
  99.1 38.4 reduce-scatter.5
where the time goes:
time: 146 us
  waiting for transfers between devices  97.7 us (67%)
  blocking collectives  17.5 us (12%)
  between operations  14.5 us (10%)
  other arithmetic  6.76 us (5%)
  matrix products  5.55 us (4%)
  local copies, waits for them, and re-layouts  2.89 us (2%)
    reduce_scatter x1, waiting for transfers between devices, on_device(): lax.psum_scatter(part_up, 'dp', scatter_dimension=0, tiled=True).astype(F32)  40.1 us
    reduce_scatter x1, waiting for transfers between devices, on_device(): lax.psum_scatter(part_down, 'dp', scatter_dimension=0, tiled=True)  38.5 us
    all_gather x1, blocking collectives, on_device(): full = lax.all_gather(packed, 'expert', axis=0, tiled=True)  17.5 us
    reduce_scatter x1, waiting for transfers between devices, on_device(): back = lax.psum_scatter(back, 'expert', scatter_dimension=0, tiled=True)  14.2 us
    ppermute x1, waiting for transfers between devices, on_device(): lax.ppermute(jnp.concatenate([active, d_hidden], axis=1), 'expert', [(i,...  4.77 us
    broadcast_in_dim x2, other arithmetic, on_device(): return (back[:, :width], back[:, width:], sum_up[None], sum_down[None])  3.4 us
  transfers between devices with their start and end apart: 4, of which 4 were waited for; matrix products, arithmetic and copies ran while one was open for 5% of the time, Pallas kernels for 0%

commit v1 on v0

--- a/solution.py
+++ b/solution.py
@@ -15,7 +15,25 @@
     hit = expert_ids[:, :, None] == lanes[None, None, :]
     gates = jnp.sum(jnp.where(hit, gate_weights.astype(F32)[:, :, None], 0.0), axis=1).astype(BF)
     packed = jnp.concatenate([tokens, out_grad, gates], axis=1)
-    full = lax.all_gather(packed, "expert", axis=0, tiled=True)
+    ways, here, hop = (lax.axis_size("expert"), lax.axis_index("expert"), packed.shape[0])
+    shape = [n * ways if d == 0 else n for d, n in enumerate(packed.shape)]
+    full_2 = lax.dynamic_update_slice_in_dim(
+        jnp.zeros(shape, packed.dtype), packed, here * hop, axis=0
+    )
+    going_up = going_down = packed
+    for far in range(1, ways // 2 + 1):
+        going_up = lax.ppermute(going_up, "expert", [(d, (d + 1) % ways) for d in range(ways)])
+        full_2 = lax.dynamic_update_slice_in_dim(
+            full_2, going_up, (here - far) % ways * hop, axis=0
+        )
+        if 2 * far < ways:
+            going_down = lax.ppermute(
+                going_down, "expert", [(d, (d - 1) % ways) for d in range(ways)]
+            )
+            full_2 = lax.dynamic_update_slice_in_dim(
+                full_2, going_down, (here + far) % ways * hop, axis=0
+            )
+    full = full_2
     x, og, gates = (full[:, :width], full[:, width : 2 * width], full[:, 2 * width :])
     gates = gates.astype(F32)
     flag = lax.dynamic_slice_in_dim(swapped, mine, 1, 0)[0] == 1

time: 146 us -> 141 us (0.966)
  blocking collectives: 17.5 us -> 0 us
  waiting for transfers between devices: 97.7 us -> 104 us
  starting transfers between devices: 0.93 us -> 6.07 us
    all_gather x1 -> x0, blocking collectives: 17.5 us -> none  [on_device(): full = lax.all_gather(packed, 'expert', axis=0, tiled=True)]
    ppermute x0 -> x3, waiting for transfers between devices: none -> 9.21 us  [the longest x2 7.75 us: on_device(): lax.ppermute(going_up, 'expert', [(d, (d + 1) % ways) for d in range(ways)])]
    ppermute x0 -> x3, starting transfers between devices: none -> 5.17 us  [the longest x2 3.08 us: on_device(): lax.ppermute(going_up, 'expert', [(d, (d + 1) % ways) for d in range(ways)])]
    reduce_scatter x1, waiting for transfers between devices: 14.2 us -> 11.7 us  [on_device(): back = lax.psum_scatter(back, 'expert', scatter_dimension=0, tiled=True)]
  transfers between devices with their start and end apart: 4 -> 7, of which waited for: 4 -> 7; matrix products, arithmetic and copies ran while one was open for 5% -> 6% of each run, Pallas kernels for 0% -> 0%
where the time goes in v1:
time: 141 us; the launch traced here: 140 us
  waiting for transfers between devices  104 us (74%)
  between operations  14.5 us (10%)
  other arithmetic  6.78 us (5%)
  starting transfers between devices  6.07 us (4%)
  matrix products  5.59 us (4%)
  local copies, waits for them, and re-layouts  2.87 us (2%)
    reduce_scatter x1, waiting for transfers between devices, on_device(): lax.psum_scatter(part_up, 'dp', scatter_dimension=0, tiled=True).astype(F32)  40.1 us
    reduce_scatter x1, waiting for transfers between devices, on_device(): lax.psum_scatter(part_down, 'dp', scatter_dimension=0, tiled=True)  38.5 us
    reduce_scatter x1, waiting for transfers between devices, on_device(): back = lax.psum_scatter(back, 'expert', scatter_dimension=0, tiled=True)  11.7 us
    ppermute x2, waiting for transfers between devices, on_device(): lax.ppermute(going_up, 'expert', [(d, (d + 1) % ways) for d in range(ways)])  7.75 us
    ppermute x1, waiting for transfers between devices, on_device(): lax.ppermute(jnp.concatenate([active, d_hidden], axis=1), 'expert', [(i,...  4.9 us
    broadcast_in_dim x2, other arithmetic, on_device(): return (back[:, :width], back[:, width:], sum_up[None], sum_down[None])  3.4 us
    ppermute x2, starting transfers between devices, on_device(): lax.ppermute(going_up, 'expert', [(d, (d + 1) % ways) for d in range(ways)])  3.08 us
  transfers between devices with their start and end apart: 7, of which 7 were waited for; matrix products, arithmetic and copies ran while one was open for 6% of the time, Pallas kernels for 0%

profile of v1, /device:TPU:0, one launch (start us, length us, event | category | flops | bytes accessed | tf_op | source)
XLA Modules:
  0.0 140.2 jit_solution(7353293040393145104)
XLA Ops:
  7.2 0.8 convert_element_type.45
  8.0 0.8 select_reduce_fusion
  8.8 0.9 pad_maximum_fusion.1
  9.7 3.1 %collective-permute-start = (bf16[16,4224]{1,0:T(8,128)(2,1)S(1)}, bf16[16,4224]{1,0:T(8,128)(2,1)S(1)}, u32[]{:S(2)}, u32[]{:S(2)}) collective-permute-start(bf16[16,4224]{1,0:T(8,128)(2,1)S(1)} %get-tuple-element.6), channel_id=1, source_target_pairs={{0,1},{1,2},{2,3},{3,0},{4,5},{5,6},{6,7},{7,4},{8,9},{9,10},{10,1... | collective-permute-start | bytes 405512 | tf_op jit(solution)/shard_map/ppermute | solution.py:25
  12.8 2.1 %collective-permute-start.1 = (bf16[16,4224]{1,0:T(8,128)(2,1)S(1)}, bf16[16,4224]{1,0:T(8,128)(2,1)S(1)}, u32[]{:S(2)}, u32[]{:S(2)}) collective-permute-start(bf16[16,4224]{1,0:T(8,128)(2,1)S(1)} %get-tuple-element.6), channel_id=1, source_target_pairs={{0,3},{1,0},{2,1},{3,2},{4,7},{5,4},{6,5},{7,6},{8,11},{9,8},{10,9... | collective-permute-start | bytes 405512 | tf_op jit(solution)/shard_map/ppermute | solution.py:30
  14.9 1.2 dynamic_slice.3
  16.8 2.4 %collective-permute-done = bf16[16,4224]{1,0:T(8,128)(2,1)S(1)} collective-permute-done((bf16[16,4224]{1,0:T(8,128)(2,1)S(1)}, bf16[16,4224]{1,0:T(8,128)(2,1)S(1)}, u32[]{:S(2)}, u32[]{:S(2)}) %collective-permute-start) | collective-permute-done | bytes 135200 | tf_op jit(solution)/shard_map/ppermute | solution.py:25
  19.2 1.5 %collective-permute-done.1 = bf16[16,4224]{1,0:T(8,128)(2,1)S(1)} collective-permute-done((bf16[16,4224]{1,0:T(8,128)(2,1)S(1)}, bf16[16,4224]{1,0:T(8,128)(2,1)S(1)}, u32[]{:S(2)}, u32[]{:S(2)}) %collective-permute-start.1) | collective-permute-done | bytes 135200 | tf_op jit(solution)/shard_map/ppermute | solution.py:30
  20.7 5.3 %collective-permute-done.2 = bf16[16,4224]{1,0:T(8,128)(2,1)S(1)} collective-permute-done((bf16[16,4224]{1,0:T(8,128)(2,1)S(1)}, bf16[16,4224]{1,0:T(8,128)(2,1)S(1)}, u32[]{:S(2)}, u32[]{:S(2)}) %collective-permute-start.2) | collective-permute-done | bytes 135200 | tf_op jit(solution)/shard_map/ppermute | solution.py:25
  26.2 0.4 select_convert_fusion
  26.6 0.6 fusion.21
  27.2 0.4 fusion.2
  27.6 0.6 convolution_convert_fusion.2
  28.2 0.8 pad_maximum_fusion
  29.2 0.8 collective-permute-start.3
  29.9 4.9 %collective-permute-done.3 = bf16[64,768]{1,0:T(8,128)(2,1)S(1)} collective-permute-done((bf16[64,768]{1,0:T(8,128)(2,1)S(1)}, bf16[64,768]{1,0:T(8,128)(2,1)S(1)}, u32[]{:S(2)}, u32[]{:S(2)}) %collective-permute-start.3) | collective-permute-done | bytes 98336 | tf_op jit(solution)/shard_map/ppermute | solution.py:53
  34.8 1.8 %convolution_convert_fusion = bf16[384,2048]{1,0:T(8,128)(2,1)} fusion(f32[64]{0:T(128)S(1)} %get-tuple-element.4, bf16[64,4224]{1,0:T(8,128)(2,1)S(1)} %constant_dynamic-update-slice_fusion, bf16[64,384]{1,0:T(8,128)(2,1)S(1)} %get-tuple-element.10, bf16[64,768]{1,0:T(8,128)(2,1)S(1)} %collective-permute-done.3, pred[]{:T(512)} %bitcast.2), kind=kOutput, calls=%fused_computation | convolution fusion | flops 101867520 | bytes 1933825 | tf_op jit(solution)/shard_map/dot_general | solution.py:68
  36.7 1.8 %convolution_convert_fusion.1 = bf16[2048,384]{1,0:T(8,128)(2,1)} fusion(bf16[64,4224]{1,0:T(8,128)(2,1)S(1)} %constant_dynamic-update-slice_fusion, bf16[64,384]{1,0:T(8,128)(2,1)S(1)} %fusion.21, bf16[64,768]{1,0:T(8,128)(2,1)S(1)} %collective-permute-done.3, pred[]{:T(512)} %bitcast.2), kind=kOutput, calls=%fused_computation.1 | convolution fusion | flops 101474304 | bytes 1933313 | tf_op jit(solution)/shard_map/dot_general | solution.py:67
  38.5 11.7 %reduce-scatter.4.cloned.1.call-done = bf16[16,4096]{1,0:T(8,128)(2,1)} async-done(((bf16[64,4096]{1,0:T(8,128)(2,1)}), bf16[16,4096]{1,0:T(8,128)(2,1)}) %reduce-scatter.4.cloned.1.call-update) | async-done | bytes 131088 | tf_op jit(solution)/shard_map/reduce_scatter | solution.py:61
  50.2 1.5 %fusion.36 = (bf16[16,2048]{1,0:T(8,128)(2,1)}, bf16[16,2048]{1,0:T(8,128)(2,1)}) fusion(bf16[16,4096]{1,0:T(8,128)(2,1)} %reduce-scatter.4.cloned.1.call-done), kind=kLoop, calls=%fused_computation.50 | loop fusion | bytes 262144 | tf_op jit(solution)/shard_map/slice | solution.py:71
  51.7 38.5 %reduce-scatter.8.cloned.1.call-done = bf16[48,2048]{1,0:T(8,128)(2,1)} async-done(((bf16[384,2048]{1,0:T(8,128)(2,1)}), bf16[48,2048]{1,0:T(8,128)(2,1)}) %reduce-scatter.8.cloned.1.call-update) | async-done | bytes 196624 | tf_op jit(solution)/shard_map/reduce_scatter | solution.py:70
  90.2 1.7 %bitcast_convert_fusion = f32[1,48,2048]{2,1,0:T(8,128)} fusion(bf16[48,2048]{1,0:T(8,128)(2,1)} %reduce-scatter.8.cloned.1.call-done), kind=kLoop, calls=%fused_computation.27 | loop fusion | flops 98304 | bytes 589824 | tf_op jit(solution)/shard_map/broadcast_in_dim | solution.py:71
  91.9 40.1 %reduce-scatter.6.cloned.1.call-done = bf16[256,384]{1,0:T(8,128)(2,1)} async-done(((bf16[2048,384]{1,0:T(8,128)(2,1)}), bf16[256,384]{1,0:T(8,128)(2,1)}) %reduce-scatter.6.cloned.1.call-update) | async-done | bytes 196624 | tf_op jit(solution)/shard_map/reduce_scatter | solution.py:69
  132.0 1.7 %bitcast_convert_fusion.1 = f32[1,256,384]{2,1,0:T(8,128)} fusion(bf16[256,384]{1,0:T(8,128)(2,1)} %reduce-scatter.6.cloned.1.call-done), kind=kLoop, calls=%fused_computation.28 | loop fusion | flops 98304 | bytes 589824 | tf_op jit(solution)/shard_map/broadcast_in_dim | solution.py:71
  (19 shorter events, 0.4 us)
Async XLA Ops:
  7.2 19.0 %copy-start = (bf16[1,2048,384]{2,1,0:T(8,128)(2,1)S(1)}, bf16[1,2048,384]{2,1,0:T(8,128)(2,1)}, u32[]{:S(2)}) copy-start(bf16[1,2048,384]{2,1,0:T(8,128)(2,1)} %param.12) | copy-start | bytes 4718596
  7.2 43.0 %reduce-scatter.4.cloned.1.call-start = ((), (), s32[]{:S(2)}) async-start(), calls=%async_computation.3 | async-start | bytes 655360 | tf_op jit(solution)/shard_map/reduce_scatter | solution.py:61
  9.7 9.5 %collective-permute-start = (bf16[16,4224]{1,0:T(8,128)(2,1)S(1)}, bf16[16,4224]{1,0:T(8,128)(2,1)S(1)}, u32[]{:S(2)}, u32[]{:S(2)}) collective-permute-start(bf16[16,4224]{1,0:T(8,128)(2,1)S(1)} %get-tuple-element.6), channel_id=1, source_target_pairs={{0,1},{1,2},{2,3},{3,0},{4,5},{5,6},{6,7},{7,4},{8,9},{9,10},{10,1... | collective-permute-start | bytes 405512 | tf_op jit(solution)/shard_map/ppermute | solution.py:25
  12.8 7.9 %collective-permute-start.1 = (bf16[16,4224]{1,0:T(8,128)(2,1)S(1)}, bf16[16,4224]{1,0:T(8,128)(2,1)S(1)}, u32[]{:S(2)}, u32[]{:S(2)}) collective-permute-start(bf16[16,4224]{1,0:T(8,128)(2,1)S(1)} %get-tuple-element.6), channel_id=1, source_target_pairs={{0,3},{1,0},{2,1},{3,2},{4,7},{5,4},{6,5},{7,6},{8,11},{9,8},{10,9... | collective-permute-start | bytes 405512 | tf_op jit(solution)/shard_map/ppermute | solution.py:30
  16.8 9.8 %copy-start.1 = (bf16[1,384,2048]{2,1,0:T(8,128)(2,1)S(1)}, bf16[1,384,2048]{2,1,0:T(8,128)(2,1)}, u32[]{:S(2)}) copy-start(bf16[1,384,2048]{2,1,0:T(8,128)(2,1)} %param.13) | copy-start | bytes 4718596
  19.2 6.8 %collective-permute-start.2 = (bf16[16,4224]{1,0:T(8,128)(2,1)S(1)}, bf16[16,4224]{1,0:T(8,128)(2,1)S(1)}, u32[]{:S(2)}, u32[]{:S(2)}) collective-permute-start(bf16[16,4224]{1,0:T(8,128)(2,1)S(1)} %collective-permute-done), channel_id=1, source_target_pairs={{0,1},{1,2},{2,3},{3,0},{4,5},{5,6},{6,7},{7,4},{8,9},{9,10},{10,1... | collective-permute-start | bytes 405512 | tf_op jit(solution)/shard_map/ppermute | solution.py:25
  29.1 61.1 %reduce-scatter.8.cloned.1.call-start = ((), (), s32[]{:S(2)}) async-start(), calls=%async_computation.5 | async-start | bytes 1769472 | tf_op jit(solution)/shard_map/reduce_scatter | solution.py:70
  29.2 5.7 %collective-permute-start.3 = (bf16[64,768]{1,0:T(8,128)(2,1)S(1)}, bf16[64,768]{1,0:T(8,128)(2,1)S(1)}, u32[]{:S(2)}, u32[]{:S(2)}) collective-permute-start(bf16[64,768]{1,0:T(8,128)(2,1)S(1)} %pad_maximum_fusion.2), channel_id=1, source_target_pairs={{0,2},{1,3},{2,0},{3,1},{4,6},{5,7},{6,4},{7,5},{8,10},{9,11},{10,... | collective-permute-start | bytes 294920 | tf_op jit(solution)/shard_map/ppermute | solution.py:53
  36.7 95.3 %reduce-scatter.6.cloned.1.call-start = ((), (), s32[]{:S(2)}) async-start(), calls=%async_computation.4 | async-start | bytes 1769472 | tf_op jit(solution)/shard_map/reduce_scatter | solution.py:69
Sparse Core Ops, SparseCore 0:
  29.2 20.9 reduce-scatter.3
  53.5 36.6 reduce-scatter.7
  93.5 38.4 reduce-scatter.5
